TPU v7x, 32 devices: a whole 2x2x4 slice. The times are simulated.
32 devices in a mesh: space: 4 (over y, core), test: 2 (over x), trial: 4 (over z).
Axes of the slice: x: 2, y: 2, z: 4, core: 2. Of those that a mesh axis runs over, the one named last changes fastest.
Arguments:
- test_modes: bfloat16 [3, 128, 16, 8, 128], P(None, 'test', 'space'), may hold values from -6 to 6
- trial_modes: bfloat16 [3, 128, 16, 8, 128], P(None, 'trial', 'space'), may hold values from -6 to 6
- volumes: float32 [16, 8, 128], P('space'), may hold values from 0.25 to 4
Outputs:
- tensor: float32 [128, 128, 128], P('space', 'test', 'trial')
All inputs are finite; a program needn't handle non-finite values.
Results may differ from a plain program's by a relative error of at most 0.0051.
Values may be sent and summed in bfloat16 or wider, within the bound.
A program may use at most 64 MiB of HBM per device.

v0:
```python
import math

import jax
import jax.numpy as jnp
from jax import lax
from jax.sharding import PartitionSpec as P


def with_halo(cells, sides, width):
    for axis, dim in sides:
        count = lax.axis_size(axis)
        ends = count - 1
        head = lax.slice_in_dim(cells, 0, width, axis=dim)
        tail = lax.slice_in_dim(cells, cells.shape[dim] - width, cells.shape[dim], axis=dim)
        cells = jnp.concatenate(
            [
                lax.ppermute(tail, axis, [(i, (i + 1) % count) for i in range(ends)]),
                cells,
                lax.ppermute(head, axis, [((i + 1) % count, i) for i in range(ends)]),
            ],
            axis=dim,
        )
    return cells


def derivatives(padded):
    field = padded.astype(jnp.float32)
    along_x = (field[:, :, 2:] - field[:, :, :-2]) * 0.5
    center = field[:, :, 1:-1]
    wide_y = jnp.pad(center, ((0, 0), (0, 0), (0, 0), (1, 1), (0, 0)))
    along_y = (wide_y[:, :, :, 2:] - wide_y[:, :, :, :-2]) * 0.5
    wide_z = jnp.pad(center, ((0, 0), (0, 0), (0, 0), (0, 0), (1, 1)))
    along_z = (wide_z[:, :, :, :, 2:] - wide_z[:, :, :, :, :-2]) * 0.5
    return jnp.stack([along_x, along_y, along_z], axis=1).astype(jnp.bfloat16)


def pick_row(array, plane, row, first):
    return lax.dynamic_index_in_dim(
        lax.dynamic_index_in_dim(array, plane, first, False), row, first, False
    )


def block_terms(mode_rows, grad_rows, weighted):
    width_j = mode_rows.shape[1]
    width_k = grad_rows.shape[2]
    planes = mode_rows.shape[2]
    rows_each = mode_rows.shape[3]

    def advance(position, running):
        plane = position // rows_each
        row = position % rows_each
        trial_block = pick_row(mode_rows, plane, row, 2)
        grad_block = pick_row(grad_rows, plane, row, 3)
        test_block = pick_row(weighted, plane, row, 2)
        convected = jnp.einsum(
            "bjc,abkc->ajkc", trial_block, grad_block, preferred_element_type=jnp.float32
        ).astype(jnp.bfloat16)
        return running + jnp.einsum(
            "aic,ajkc->jik", test_block, convected, preferred_element_type=jnp.float32
        )

    running = jnp.zeros((width_j, weighted.shape[1], width_k), jnp.float32)
    return lax.fori_loop(0, planes * rows_each, advance, running)


def finish(partial_value, factor):
    return lax.psum_scatter(partial_value, "space", scatter_dimension=0, tiled=True) * factor


def shards(test_modes, trial_modes, volumes):
    cell_count = trial_modes.shape[2] * trial_modes.shape[3] * trial_modes.shape[4]
    factor = 1.0 / (4.0 * math.sqrt(cell_count * lax.axis_size("space")))
    padded = with_halo(trial_modes, (("space", 2),), 1)
    gradients = derivatives(padded)
    weighted = (test_modes.astype(jnp.float32) * volumes).astype(jnp.bfloat16)
    all_modes = lax.all_gather(trial_modes, "trial", axis=1, tiled=True)
    partial_value = block_terms(all_modes, gradients, weighted)
    return finish(partial_value, factor)


def solution(mesh):
    return jax.shard_map(
        shards,
        mesh=mesh,
        in_specs=(
            P(None, "test", "space", None, None),
            P(None, "trial", "space", None, None),
            P("space", None, None),
        ),
        out_specs=P("space", "test", "trial"),
        check_vma=False,
    )
```

profile of v0, /device:TPU:1, one launch (start us, length us, event | category | flops | bytes accessed | tf_op | source)
XLA Modules:
  0.0 494.6 jit_solution(17694569836780700813)
XLA Ops:
  10.1 4.5 collective-permute-start
  25.0 49.7 %all-gather.2.cloned.1.call-done = bf16[3,128,4,8,128]{4,1,0,3,2:T(8,128)(2,1)} async-done(((bf16[3,32,4,8,128]{4,1,0,3,2:T(8,128)(2,1)}), bf16[3,128,4,8,128]{4,1,0,3,2:T(8,128)(2,1)}) %all-gather.2.cloned.1.call-update) | async-done | bytes 3145744 | tf_op jit(solution)/shard_map/all_gather | solution.py:76
  74.7 376.8 %while.17 = (s32[]{:T(128)}, f32[128,64,32]{0,1,2:T(8,128)}, bf16[3,3,32,4,8,128]{5,2,1,0,4,3:T(8,128)(2,1)}, bf16[3,128,4,8,128]{4,1,0,3,2:T(8,128)(2,1)}, bf16...) while((s32[]{:T(128)}, f32[128,64,32]{0,1,2:T(8,128)}, ...), condition=%wide.region_1.2_spmd.clone, body=%wide.region_0.1_spmd.clone.sunk | while | flops 211288080 | bytes 15589742 | solution.py:63
  79.4 3.8 copy.26
  90.7 3.8 copy.26
  102.5 3.8 copy.26
  114.3 3.8 copy.26
  126.1 3.8 copy.26
  137.9 3.8 copy.26
  149.7 3.8 copy.26
  161.5 3.8 copy.26
  173.2 3.8 copy.26
  185.0 3.8 copy.26
  196.8 3.8 copy.26
  208.6 3.8 copy.26
  220.4 3.8 copy.26
  244.0 3.8 copy.26
  255.8 3.8 copy.26
  279.3 3.8 copy.26
  291.1 3.8 copy.26
  302.9 3.8 copy.26
  314.7 3.8 copy.26
  326.5 3.8 copy.26
  338.3 3.8 copy.26
  350.1 3.8 copy.26
  361.9 3.8 copy.26
  373.7 3.8 copy.26
  385.5 3.8 copy.26
  397.2 3.8 copy.26
  409.0 3.8 copy.26
  451.5 4.0 copy.15
  455.6 30.3 %reduce-scatter.2.cloned.1.call-done = f32[32,64,32]{1,2,0:T(8,128)} async-done(((f32[128,64,32]{1,2,0:T(8,128)}), f32[32,64,32]{1,2,0:T(8,128)}) %reduce-scatter.2.cloned.1.call-update) | async-done | bytes 262160 | tf_op jit(solution)/shard_map/reduce_scatter | solution.py:67
  (219 shorter events, 289.4 us)
Async XLA Ops:
  6.5 10.1 %copy-start.1 = (bf16[3,64,4,8,128]{4,3,2,1,0:T(8,128)(2,1)S(1)}, bf16[3,64,4,8,128]{4,3,2,1,0:T(8,128)(2,1)}, u32[]{:S(2)}) copy-start(bf16[3,64,4,8,128]{4,3,2,1,0:T(8,128)(2,1)} %param.5) | copy-start | bytes 4718596
  6.5 10.1 %copy-start.2 = (f32[4,8,128]{2,1,0:T(8,128)S(1)}, f32[4,8,128]{2,1,0:T(8,128)}, u32[]{:S(2)}) copy-start(f32[4,8,128]{2,1,0:T(8,128)} %param.7) | copy-start | bytes 49156
  6.5 68.2 %all-gather.2.cloned.1.call-start = ((), (), s32[]{:S(2)}) async-start(), calls=%async_computation.1 | async-start | bytes 3932160 | tf_op jit(solution)/shard_map/all_gather | solution.py:76
  9.0 476.8 %reduce-scatter.2.cloned.1.call-start = ((), (), s32[]{:S(2)}) async-start(), calls=%async_computation.2 | async-start | bytes 2621440 | tf_op jit(solution)/shard_map/reduce_scatter | solution.py:67
  10.1 8.4 %collective-permute-start = (bf16[3,32,1,8,128]{4,1,0,3,2:T(8,128)(2,1)S(1)}, bf16[3,32,1,8,128]{4,1,0,3,2:T(8,128)(2,1)S(1)}, u32[]{:S(2)}, u32[]{:S(2)}) collective-permute-start(bf16[3,32,1,8,128]{4,1,0,3,2:T(8,128)(2,1)S(1)} %get-tuple-element.202), channel_id=1, source_target_pairs={{0,8},{8,16},{16,24},{1,9},{9,17},{17,25},{2,10},{10,18},{18,26},{... | collective-permute-start | bytes 589832 | tf_op jit(solution)/shard_map/ppermute | solution.py:17
  14.7 7.0 %collective-permute-start.1 = (bf16[3,32,1,8,128]{4,1,0,3,2:T(8,128)(2,1)S(1)}, bf16[3,32,1,8,128]{4,1,0,3,2:T(8,128)(2,1)S(1)}, u32[]{:S(2)}, u32[]{:S(2)}) collective-permute-start(bf16[3,32,1,8,128]{4,1,0,3,2:T(8,128)(2,1)S(1)} %get-tuple-element.203), channel_id=1, source_target_pairs={{8,0},{16,8},{24,16},{9,1},{17,9},{25,17},{10,2},{18,10},{26,18},{... | collective-permute-start | bytes 589832 | tf_op jit(solution)/shard_map/ppermute | solution.py:19
  16.6 5.0 %copy-start = (bf16[3,32,4,8,128]{4,1,0,3,2:T(8,128)(2,1)S(1)}, bf16[3,32,4,8,128]{4,1,0,3,2:T(8,128)(2,1)}, u32[]{:S(2)}) copy-start(bf16[3,32,4,8,128]{4,1,0,3,2:T(8,128)(2,1)} %copy.8) | copy-start | bytes 2359300
Sparse Core Ops, SparseCore 0:
  9.1 65.5 all-gather.1
  455.7 30.0 reduce-scatter.1
where the time goes:
time: 500 us; the launch traced here: 495 us
  local copies, waits for them, and re-layouts  198 us (40%)
  matrix products  186 us (37%)
  waiting for transfers between devices  83.2 us (17%)
  between operations  13.5 us (3%)
  other arithmetic  7.03 us (1%)
  starting transfers between devices  6.5 us (1%)
    dot_general x32, local copies, waits for them, and re-layouts, advance(): jnp.einsum('bjc,abkc->ajkc', trial_block, grad_block, preferred_element_t...  121 us
    dot_general x32, matrix products, advance(): jnp.einsum('aic,ajkc->jik', test_block, convected, preferred_element_type...  106 us
    dot_general x32, matrix products, advance(): jnp.einsum('bjc,abkc->ajkc', trial_block, grad_block, preferred_element_t...  79.3 us
    squeeze x128, local copies, waits for them, and re-layouts, pick_row(): lax.dynamic_index_in_dim(lax.dynamic_index_in_dim(array, plane, first, Fa...  69.2 us
    all_gather x1, waiting for transfers between devices, shards(): all_modes = lax.all_gather(trial_modes, 'trial', axis=1, tiled=True)  49.7 us
    reduce_scatter x1, waiting for transfers between devices, finish(): lax.psum_scatter(partial_value, 'space', scatter_dimension=0, tiled=True)  30.3 us
  transfers between devices with their start and end apart: 4, of which 3 were waited for; matrix products, arithmetic and copies ran while one was open for 1% of the time, Pallas kernels for 0%

commit v1 on v0

v1 whole, which is shorter than its diff:
```python
import functools
import math

import jax
import jax.numpy as jnp
from jax import lax
from jax.experimental import pallas as pl
from jax.experimental.pallas import tpu as pltpu
from jax.sharding import PartitionSpec as P

GROUP = 8
MIXED = jnp.float32


def slope(later, earlier):
    return (later.astype(jnp.float32) - earlier.astype(jnp.float32)) * 0.5


def gradients_of_plane(before, here, after):
    rows, parts, modes, lanes = here.shape
    none = jnp.zeros((1, parts, modes, lanes), here.dtype)
    along_x = slope(after, before)
    along_y = slope(
        jnp.concatenate([here[1:], none], axis=0), jnp.concatenate([none, here[:-1]], axis=0)
    )
    wide = here.astype(jnp.float32).reshape(rows * parts * modes, lanes)
    lane = lax.broadcasted_iota(jnp.int32, wide.shape, 1)
    following = jnp.where(lane == lanes - 1, 0.0, pltpu.roll(wide, lanes - 1, 1))
    previous = jnp.where(lane == 0, 0.0, pltpu.roll(wide, 1, 1))
    along_z = ((following - previous) * 0.5).reshape(here.shape)
    return along_x, along_y, along_z


def pair_rows(weighted_ref, grad_ref, plane, first_row, rows, first_mode):
    columns = []
    for row in range(rows):
        grads = [[grad_ref[plane, first_row + row, a, b] for b in range(3)] for a in range(3)]
        per_mode = []
        for mode in range(GROUP):
            w = [
                jnp.broadcast_to(
                    weighted_ref[plane, first_row + row, a, pl.ds(first_mode + mode, 1), :],
                    grads[0][0].shape,
                ).astype(MIXED)
                for a in range(3)
            ]
            per_mode.append(
                [
                    (w[0] * grads[0][b] + w[1] * grads[1][b] + w[2] * grads[2][b]).astype(jnp.bfloat16)
                    for b in range(3)
                ]
            )
        for b in range(3):
            columns.append(jnp.concatenate([m[b] for m in per_mode], axis=0))
    return jnp.concatenate(columns, axis=1)


def kernel(padded_ref, all_ref, weighted_ref, out_ref, grad_ref, total_ref):
    planes, rows_each = all_ref.shape[0], all_ref.shape[1]
    modes = padded_ref.shape[3]
    tests = weighted_ref.shape[3]

    @pl.loop(0, planes)
    def _(plane):
        found = gradients_of_plane(padded_ref[plane], padded_ref[plane + 1], padded_ref[plane + 2])
        for b in range(3):
            grad_ref[plane, :, :, b] = found[b].astype(jnp.bfloat16).astype(MIXED)

    total_ref[...] = jnp.zeros_like(total_ref)
    pairs = rows_each // 2
    unroll = 4
    span = GROUP * unroll

    @pl.loop(0, planes * pairs * (tests // span))
    def _(step):
        part = step % (tests // span)
        place = step // (tests // span)
        plane, row = place // pairs, (place % pairs) * 2
        trial = jnp.concatenate(
            [all_ref[plane, row + r, b] for r in range(2) for b in range(3)], axis=1
        )
        for u in range(unroll):
            first = part * span + u * GROUP
            lhs = pair_rows(weighted_ref, grad_ref, plane, row, 2, first)
            where = pl.ds(pl.multiple_of(first * modes, GROUP * modes), GROUP * modes)
            total_ref[where, :] += lax.dot_general(
                lhs, trial, (((1,), (1,)), ((), ())), preferred_element_type=jnp.float32
            )

    out_ref[...] = total_ref[...].T


def shards(test_modes, trial_modes, volumes):
    cell_count = trial_modes.shape[2] * trial_modes.shape[3] * trial_modes.shape[4]
    count = lax.axis_size("space")
    factor = 1.0 / (4.0 * math.sqrt(cell_count * count))
    order = (2, 3, 0, 1, 4)
    own = jnp.transpose(trial_modes, order)
    weighted = jnp.transpose(
        (test_modes.astype(jnp.float32) * volumes).astype(jnp.bfloat16), order
    ).astype(jnp.float32)
    ends = count - 1
    padded = jnp.concatenate(
        [
            lax.ppermute(own[-1:], "space", [(i, i + 1) for i in range(ends)]),
            own,
            lax.ppermute(own[:1], "space", [(i + 1, i) for i in range(ends)]),
        ],
        axis=0,
    )
    every = lax.all_gather(own, "trial", axis=3, tiled=True)
    planes, rows_each, _, modes, lanes = own.shape
    tests = weighted.shape[3]
    total = pl.pallas_call(
        kernel,
        out_shape=jax.ShapeDtypeStruct((every.shape[3], tests * modes), jnp.float32),
        in_specs=[pl.BlockSpec(memory_space=pltpu.VMEM)] * 3,
        out_specs=pl.BlockSpec(memory_space=pltpu.VMEM),
        scratch_shapes=[
            pltpu.VMEM((planes, rows_each, 3, 3, modes, lanes), MIXED),
            pltpu.VMEM((tests * modes, every.shape[3]), jnp.float32),
        ],
        compiler_params=pltpu.CompilerParams(vmem_limit_bytes=48 * 2**20),
    )(padded, every, weighted)
    mine = lax.psum_scatter(total, "space", scatter_dimension=0, tiled=True) * factor
    return mine.reshape(mine.shape[0], tests, modes)


def solution(mesh):
    return jax.shard_map(
        shards,
        mesh=mesh,
        in_specs=(
            P(None, "test", "space", None, None),
            P(None, "trial", "space", None, None),
            P("space", None, None),
        ),
        out_specs=P("space", "test", "trial"),
        check_vma=False,
    )
```

time: 500 us -> 140 us (0.28)
  local copies, waits for them, and re-layouts: 198 us -> 6.88 us
  matrix products: 186 us -> 0 us
  Pallas kernels: 0 us -> 29.7 us
    dot_general x64 -> x0, matrix products: 186 us -> none  [the longest x32 106 us: advance(): jnp.einsum('aic,ajkc->jik', test_block, convected, preferred_element_type...]
    dot_general x32 -> x0, local copies, waits for them, and re-layouts: 121 us -> none  [advance(): jnp.einsum('bjc,abkc->ajkc', trial_block, grad_block, preferred_element_t...]
    squeeze x128 -> x0, local copies, waits for them, and re-layouts: 69.2 us -> none  [pick_row(): lax.dynamic_index_in_dim(lax.dynamic_index_in_dim(array, plane, first, Fa...]
    pallas_call x0 -> x1, Pallas kernels: none -> 29.7 us  [shards(): pl.pallas_call(kernel, out_shape=jax.ShapeDtypeStruct((every.shape[3], te...]
    reduce_scatter x1, waiting for transfers between devices: 30.3 us -> 23.7 us  [shards(): lax.psum_scatter(total, 'space', scatter_dimension=0, tiled=True) * factor]
  transfers between devices with their start and end apart: 4 -> 4, of which waited for: 3 -> 3; matrix products, arithmetic and copies ran while one was open for 1% -> 2% of each run, Pallas kernels for 0% -> 0%
where the time goes in v1:
time: 140 us; the launch traced here: 139 us
  waiting for transfers between devices  79.4 us (57%)
  Pallas kernels  29.7 us (21%)
  between operations  13.5 us (10%)
  local copies, waits for them, and re-layouts  6.88 us (5%)
  starting transfers between devices  6.63 us (5%)
  other arithmetic  3.29 us (2%)
    all_gather x1, waiting for transfers between devices, shards(): every = lax.all_gather(own, 'trial', axis=3, tiled=True)  52.8 us
    pallas_call x1, Pallas kernels, shards(): pl.pallas_call(kernel, out_shape=jax.ShapeDtypeStruct((every.shape[3], te...  29.7 us
    reduce_scatter x1, waiting for transfers between devices, shards(): lax.psum_scatter(total, 'space', scatter_dimension=0, tiled=True) * factor  23.7 us
    ppermute x1, starting transfers between devices, shards(): lax.ppermute(own[-1:], 'space', [(i, i + 1) for i in range(ends)])  4.54 us
    unnamed x9, local copies, waits for them, and re-layouts  4.37 us
    ppermute x1, waiting for transfers between devices, shards(): lax.ppermute(own[:1], 'space', [(i + 1, i) for i in range(ends)])  2.85 us
  transfers between devices with their start and end apart: 4, of which 3 were waited for; matrix products, arithmetic and copies ran while one was open for 2% of the time, Pallas kernels for 0%

profile of v1, /device:TPU:1, one launch (start us, length us, event | category | flops | bytes accessed | tf_op | source)
XLA Modules:
  0.0 139.3 jit_solution(43029508368248617)
XLA Ops:
  6.5 0.0 copy-start.3
  6.5 0.0 copy-start.2
  6.5 0.0 all-gather.2.cloned.1.call-start
  6.5 2.5 %copy.12 = bf16[3,32,4,8,128]{4,1,0,3,2:T(8,128)(2,1)} copy(bf16[3,32,4,8,128]{4,3,2,1,0:T(8,128)(2,1)} %param.4) | data formatting | bytes 1572864 | tf_op args[1]
  9.0 0.0 all-gather.2.cloned.1.call-update
  9.0 0.0 reduce-scatter.2.cloned.1.call-start
  9.1 1.0 fusion
  10.1 4.5 %collective-permute-start = (bf16[1,8,3,32,128]{4,3,2,1,0:T(8,128)(2,1)S(1)}, bf16[1,8,3,32,128]{4,3,2,1,0:T(8,128)(2,1)S(1)}, u32[]{:S(2)}, u32[]{:S(2)}) collective-permute-start(bf16[1,8,3,32,128]{4,3,2,1,0:T(8,128)(2,1)S(1)} %get-tuple-element.5), channel_id=1, source_target_pairs={{0,8},{8,16},{16,24},{1,9},{9,17},{17,25},{2,10},{10,18},{18,26},{... | collective-permute-start | bytes 589832 | tf_op jit(solution)/shard_map/ppermute | solution.py:105
  14.7 0.0 copy-start.1
  14.7 2.1 %collective-permute-start.1 = (bf16[1,8,3,32,128]{4,3,2,1,0:T(8,128)(2,1)S(1)}, bf16[1,8,3,32,128]{4,3,2,1,0:T(8,128)(2,1)S(1)}, u32[]{:S(2)}, u32[]{:S(2)}) collective-permute-start(bf16[1,8,3,32,128]{4,3,2,1,0:T(8,128)(2,1)S(1)} %get-tuple-element.6), channel_id=1, source_target_pairs={{8,0},{16,8},{24,16},{9,1},{17,9},{25,17},{10,2},{18,10},{26,18},{... | collective-permute-start | bytes 589832 | tf_op jit(solution)/shard_map/ppermute | solution.py:107
  16.7 0.0 copy-done.3
  16.8 0.0 copy-done.2
  16.8 2.2 %convert_bitcast_fusion.weighted_ref = f32[4,8,3,64,128]{4,3,2,1,0:T(8,128)} fusion(bf16[3,64,4,8,128]{4,3,2,1,0:T(8,128)(2,1)S(1)} %copy-done.2, f32[4,8,128]{2,1,0:T(8,128)S(1)} %copy-done.3), kind=kLoop, calls=%fused_computation | loop fusion | flops 3145728 | bytes 4734976 | tf_op jit(solution)/shard_map/convert_element_type | solution.py:101
  19.0 0.0 collective-permute-done
  19.0 2.9 %collective-permute-done.1 = bf16[1,8,3,32,128]{4,3,2,1,0:T(8,128)(2,1)S(1)} collective-permute-done((bf16[1,8,3,32,128]{4,3,2,1,0:T(8,128)(2,1)S(1)}, bf16[1,8,3,32,128]{4,3,2,1,0:T(8,128)(2,1)S(1)}, u32[]{:S(2)}, u32[]{:S(2)}) %collective-permute-start.1) | collective-permute-done | bytes 196640 | tf_op jit(solution)/shard_map/ppermute | solution.py:107
  21.8 0.0 copy-done.1
  21.8 0.1 pad_maximum_fusion.padded_ref
  22.0 52.8 %all-gather.2.cloned.1.call-done.all_ref = bf16[4,8,3,128,128]{4,3,2,1,0:T(8,128)(2,1)} async-done(((bf16[4,8,3,32,128]{4,3,2,1,0:T(8,128)(2,1)}), bf16[4,8,3,128,128]{4,3,2,1,0:T(8,128)(2,1)}) %all-gather.2.cloned.1.call-update) | async-done | bytes 3145744 | tf_op jit(solution)/shard_map/all_gather | solution.py:111
  74.7 0.0 copy-start
  74.7 1.9 %copy-done = bf16[4,8,3,128,128]{4,3,2,1,0:T(8,128)(2,1)S(1)} copy-done((bf16[4,8,3,128,128]{4,3,2,1,0:T(8,128)(2,1)S(1)}, bf16[4,8,3,128,128]{4,3,2,1,0:T(8,128)(2,1)}, u32[]{:S(2)}) %copy-start) | copy-done | bytes 3145752
  76.6 29.7 %shard_map.37 = f32[128,2048]{1,0:T(8,128)} custom-call(bf16[6,8,3,32,128]{4,3,2,1,0:T(8,128)(2,1)S(1)} %pad_maximum_fusion.padded_ref, bf16[4,8,3,128,128]{4,3,2,1,0:T(8,128)(2,1)S(1)} %copy-done, f32[4,8,3,64,128]{4,3,2,1,0:T(8,128)} %convert_bitcast_fusion.weighted_ref), custom_call_target="tpu_custom_call" | custom-call | tf_op jit(solution)/shard_map/pallas_call | solution.py:114
  106.3 0.0 reduce-scatter.2.cloned.1.call-update
  106.3 23.7 %reduce-scatter.2.cloned.1.call-done = f32[32,2048]{1,0:T(8,128)} async-done(((f32[128,2048]{1,0:T(8,128)}), f32[32,2048]{1,0:T(8,128)}) %reduce-scatter.2.cloned.1.call-update) | async-done | bytes 262160 | tf_op jit(solution)/shard_map/reduce_scatter | solution.py:125
  130.0 1.0 broadcast_multiply_fusion
  131.0 0.3 reshape.4
  131.4 1.1 copy.9
Async XLA Ops:
  6.5 10.2 %copy-start.3 = (f32[4,8,128]{2,1,0:T(8,128)S(1)}, f32[4,8,128]{2,1,0:T(8,128)}, u32[]{:S(2)}) copy-start(f32[4,8,128]{2,1,0:T(8,128)} %param.5) | copy-start | bytes 49156
  6.5 10.2 %copy-start.2 = (bf16[3,64,4,8,128]{4,3,2,1,0:T(8,128)(2,1)S(1)}, bf16[3,64,4,8,128]{4,3,2,1,0:T(8,128)(2,1)}, u32[]{:S(2)}) copy-start(bf16[3,64,4,8,128]{4,3,2,1,0:T(8,128)(2,1)} %param.3) | copy-start | bytes 4718596
  6.5 68.2 %all-gather.2.cloned.1.call-start = ((), (), s32[]{:S(2)}) async-start(), calls=%async_computation.1 | async-start | bytes 3932160 | tf_op jit(solution)/shard_map/all_gather | solution.py:111
  9.0 121.0 %reduce-scatter.2.cloned.1.call-start = ((), (), s32[]{:S(2)}) async-start(), calls=%async_computation.2 | async-start | bytes 1310720 | tf_op jit(solution)/shard_map/reduce_scatter | solution.py:125
  10.1 8.8 %collective-permute-start = (bf16[1,8,3,32,128]{4,3,2,1,0:T(8,128)(2,1)S(1)}, bf16[1,8,3,32,128]{4,3,2,1,0:T(8,128)(2,1)S(1)}, u32[]{:S(2)}, u32[]{:S(2)}) collective-permute-start(bf16[1,8,3,32,128]{4,3,2,1,0:T(8,128)(2,1)S(1)} %get-tuple-element.5), channel_id=1, source_target_pairs={{0,8},{8,16},{16,24},{1,9},{9,17},{17,25},{2,10},{10,18},{18,26},{... | collective-permute-start | bytes 589832 | tf_op jit(solution)/shard_map/ppermute | solution.py:105
  14.7 7.1 %copy-start.1 = (bf16[3,32,4,8,128]{4,1,0,3,2:T(8,128)(2,1)S(1)}, bf16[3,32,4,8,128]{4,1,0,3,2:T(8,128)(2,1)}, u32[]{:S(2)}) copy-start(bf16[3,32,4,8,128]{4,1,0,3,2:T(8,128)(2,1)} %copy.12) | copy-start | bytes 2359300
  14.7 7.1 %collective-permute-start.1 = (bf16[1,8,3,32,128]{4,3,2,1,0:T(8,128)(2,1)S(1)}, bf16[1,8,3,32,128]{4,3,2,1,0:T(8,128)(2,1)S(1)}, u32[]{:S(2)}, u32[]{:S(2)}) collective-permute-start(bf16[1,8,3,32,128]{4,3,2,1,0:T(8,128)(2,1)S(1)} %get-tuple-element.6), channel_id=1, source_target_pairs={{8,0},{16,8},{24,16},{9,1},{17,9},{25,17},{10,2},{18,10},{26,18},{... | collective-permute-start | bytes 589832 | tf_op jit(solution)/shard_map/ppermute | solution.py:107
  74.7 1.9 %copy-start = (bf16[4,8,3,128,128]{4,3,2,1,0:T(8,128)(2,1)S(1)}, bf16[4,8,3,128,128]{4,3,2,1,0:T(8,128)(2,1)}, u32[]{:S(2)}) copy-start(bf16[4,8,3,128,128]{4,3,2,1,0:T(8,128)(2,1)} %all-gather.2.cloned.1.call-done.all_ref) | copy-start | bytes 9437188
Sparse Core Ops, SparseCore 0:
  9.2 65.5 all-gather.1
  106.4 23.5 reduce-scatter.1

commit v2 on v1

--- a/solution.py
+++ b/solution.py
@@ -10,6 +10,7 @@
 
 GROUP = 8
 MIXED = jnp.float32
+MESH = pl.DeviceIdType.MESH
 
 
 def slope(later, earlier):
@@ -55,10 +56,177 @@
     return jnp.concatenate(columns, axis=1)
 
 
-def kernel(padded_ref, all_ref, weighted_ref, out_ref, grad_ref, total_ref):
-    planes, rows_each = all_ref.shape[0], all_ref.shape[1]
-    modes = padded_ref.shape[3]
+def kernel(
+    factor, own_ref, test_ref, out_ref,
+    padded_ref, all_ref, weighted_ref, grad_ref, total_ref, turned_ref, send_ref, got_ref,
+    halo_send, halo_recv, right_send, left_send, line_recv, cross_send, cross_recv, sum_send, sum_recv,
+):
+    planes, rows_each, _, modes, lanes = own_ref.shape
     tests = weighted_ref.shape[3]
+    s, t, z = lax.axis_index("space"), lax.axis_index("test"), lax.axis_index("trial")
+    ns, nt, nz = lax.axis_size("space"), lax.axis_size("test"), lax.axis_size("trial")
+    share = rows_each // nt
+    pairs = rows_each // 2
+    unroll = 4
+    span = GROUP * unroll
+    parts = tests // span
+    every = out_ref.shape[0] * ns
+    piece = out_ref.shape[0]
+
+    def block(plane, source, part):
+        return all_ref.at[plane, source, pl.ds(part * share, share)]
+
+    def along_line(plane, source, target, sems):
+        return pltpu.make_async_remote_copy(
+            block(plane, source, t), block(plane, source, t),
+            sems.at[plane, source], line_recv.at[plane, source],
+            device_id=(s, t, target), device_id_type=MESH,
+        )
+
+    def to_right(plane, source):
+        return along_line(plane, source, z + 1, right_send)
+
+    def to_left(plane, source):
+        return along_line(plane, source, z - 1, left_send)
+
+    def across(plane, source, sender, target):
+        return pltpu.make_async_remote_copy(
+            block(plane, source, sender), block(plane, source, sender),
+            cross_send.at[plane, source, target], cross_recv.at[plane, source, sender],
+            device_id=(s, target, z), device_id_type=MESH,
+        )
+
+    def halo(side):
+        return pltpu.make_async_remote_copy(
+            padded_ref.at[planes if side == 0 else 1], padded_ref.at[0 if side == 0 else planes + 1],
+            halo_send.at[side], halo_recv.at[side],
+            device_id=(s + 1 if side == 0 else s - 1, t, z), device_id_type=MESH,
+        )
+
+    def partial_to(part, peer):
+        return pltpu.make_async_remote_copy(
+            send_ref.at[part, peer], got_ref.at[part, s],
+            sum_send.at[part, peer], sum_recv.at[part, s],
+            device_id=(peer, t, z), device_id_type=MESH,
+        )
+
+    def partial_from(part, peer):
+        return pltpu.make_async_remote_copy(
+            send_ref.at[part, peer], got_ref.at[part, peer],
+            sum_send.at[part, peer], sum_recv.at[part, peer],
+            device_id=(peer, t, z), device_id_type=MESH,
+        )
+
+    barrier = pltpu.get_barrier_semaphore()
+
+    @pl.loop(1, ns)
+    def _(d):
+        pl.semaphore_signal(barrier, inc=1, device_id=(lax.rem(s + d, ns), t, z), device_id_type=MESH)
+
+    for d in range(1, nt):
+        pl.semaphore_signal(barrier, inc=1, device_id=(s, lax.rem(t + d, nt), z), device_id_type=MESH)
+
+    @pl.when(z > 0)
+    def _():
+        pl.semaphore_signal(barrier, inc=1, device_id=(s, t, z - 1), device_id_type=MESH)
+
+    @pl.when(z < nz - 1)
+    def _():
+        pl.semaphore_signal(barrier, inc=1, device_id=(s, t, z + 1), device_id_type=MESH)
+
+    @pl.loop(0, planes)
+    def _(plane):
+        here = own_ref[plane]
+        padded_ref[plane + 1] = here
+        all_ref[plane, z] = here
+
+    sides = jnp.where(z > 0, 1, 0) + jnp.where(z < nz - 1, 1, 0)
+    pl.semaphore_wait(barrier, ns - 1 + nt - 1 + sides)
+
+    def send_own(plane):
+        @pl.when(z < nz - 1)
+        def _():
+            to_right(plane, z).start()
+
+        @pl.when(z > 0)
+        def _():
+            to_left(plane, z).start()
+
+    def pass_on(plane, hop):
+        before, after = z - hop, z + hop
+
+        @pl.when(before >= 0)
+        def _():
+            to_right(plane, before).wait_recv()
+
+            @pl.when(z < nz - 1)
+            def _():
+                to_right(plane, before).start()
+
+            for d in range(1, nt):
+                across(plane, before, t, lax.rem(t + d, nt)).start()
+
+        @pl.when(after < nz)
+        def _():
+            to_left(plane, after).wait_recv()
+
+            @pl.when(z > 0)
+            def _():
+                to_left(plane, after).start()
+
+            for d in range(1, nt):
+                across(plane, after, t, lax.rem(t + d, nt)).start()
+
+    def slot(plane, hop):
+        @pl.when((hop == 0) & (plane + 1 < planes))
+        def _():
+            send_own(plane + 1)
+
+        @pl.when(hop > 0)
+        def _():
+            pass_on(plane, hop)
+
+    def wait_across(plane):
+        for d in range(1, nz):
+            source = lax.rem(z + d, nz)
+            for e in range(1, nt):
+                across(plane, source, lax.rem(t + e, nt), t).wait_recv()
+
+    send_own(0)
+
+    @pl.when(s < ns - 1)
+    def _():
+        halo(0).start()
+
+    @pl.when(s > 0)
+    def _():
+        halo(1).start()
+
+    slot(0, 0)
+
+    @pl.when(s == 0)
+    def _():
+        padded_ref[0] = jnp.zeros(padded_ref.shape[1:], padded_ref.dtype)
+
+    @pl.when(s == ns - 1)
+    def _():
+        padded_ref[planes + 1] = jnp.zeros(padded_ref.shape[1:], padded_ref.dtype)
+
+    @pl.loop(0, planes)
+    def _(plane):
+        weighted_ref[plane] = test_ref[plane].astype(jnp.float32)
+
+    total_ref[...] = jnp.zeros_like(total_ref)
+    for hop in range(1, nz):
+        slot(0, hop)
+
+    @pl.when(s > 0)
+    def _():
+        halo(0).wait_recv()
+
+    @pl.when(s < ns - 1)
+    def _():
+        halo(1).wait_recv()
 
     @pl.loop(0, planes)
     def _(plane):
@@ -66,18 +234,36 @@
         for b in range(3):
             grad_ref[plane, :, :, b] = found[b].astype(jnp.bfloat16).astype(MIXED)
 
-    total_ref[...] = jnp.zeros_like(total_ref)
-    pairs = rows_each // 2
-    unroll = 4
-    span = GROUP * unroll
-
-    @pl.loop(0, planes * pairs * (tests // span))
+    def flush(part):
+        rows = span * modes
+        value = total_ref[pl.ds(pl.multiple_of(part * rows, rows), rows), :].T
+        for peer in range(ns):
+            turned_ref[part, peer] = value[peer * piece : (peer + 1) * piece]
+            send_ref[part, peer] = value[peer * piece : (peer + 1) * piece].astype(jnp.bfloat16)
+
+        @pl.loop(1, ns)
+        def _(d):
+            partial_to(part, lax.rem(s + d, ns)).start()
+
+    @pl.loop(0, planes * pairs * parts)
     def _(step):
-        part = step % (tests // span)
-        place = step // (tests // span)
-        plane, row = place // pairs, (place % pairs) * 2
+        plane, m = step // (pairs * parts), step % (pairs * parts)
+        last = plane == planes - 1
+        q = jnp.where(last, m % pairs, m // parts)
+        part = jnp.where(last, m // pairs, m % parts)
+        row = lax.rem(t * share + q * 2, rows_each)
+
+        @pl.when(m == jnp.where(last, pairs // nt, pairs // nt * parts))
+        def _():
+            wait_across(plane)
+
         trial = jnp.concatenate(
-            [all_ref[plane, row + r, b] for r in range(2) for b in range(3)], axis=1
+            [
+                jnp.concatenate([all_ref[plane, source, row + r, b] for source in range(nz)], axis=0)
+                for r in range(2)
+                for b in range(3)
+            ],
+            axis=1,
         )
         for u in range(unroll):
             first = part * span + u * GROUP
@@ -87,43 +273,102 @@
                 lhs, trial, (((1,), (1,)), ((), ())), preferred_element_type=jnp.float32
             )
 
-    out_ref[...] = total_ref[...].T
+        @pl.when((plane + 1 < planes) & (m % parts == parts - 1))
+        def _():
+            @pl.loop(m // parts * nz // pairs, (m // parts + 1) * nz // pairs)
+            def _(hop):
+                slot(plane + 1, hop)
+
+        @pl.when(last & (m % pairs == pairs - 1))
+        def _():
+            flush(part)
+
+    width = span * modes
+    for part in range(parts):
+        @pl.loop(1, ns)
+        def _(d):
+            peer = lax.rem(s + d, ns)
+            partial_from(part, peer).wait_recv()
+            turned_ref[part, s] += got_ref[part, peer].astype(jnp.float32)
+
+        out_ref[:, part * width : (part + 1) * width] = turned_ref[part, s] * factor
+
+    @pl.loop(0, planes)
+    def _(plane):
+        @pl.loop(0, nz)
+        def _(source):
+            @pl.when((source <= z) & (z < nz - 1))
+            def _():
+                to_right(plane, source).wait_send()
+
+            @pl.when((source >= z) & (z > 0))
+            def _():
+                to_left(plane, source).wait_send()
+
+            @pl.when(source != z)
+            def _():
+                for d in range(1, nt):
+                    across(plane, source, t, lax.rem(t + d, nt)).wait_send()
+
+    @pl.when(s < ns - 1)
+    def _():
+        halo(0).wait_send()
+
+    @pl.when(s > 0)
+    def _():
+        halo(1).wait_send()
+
+    for part in range(parts):
+        @pl.loop(1, ns)
+        def _(d):
+            partial_to(part, lax.rem(s + d, ns)).wait_send()
 
 
 def shards(test_modes, trial_modes, volumes):
     cell_count = trial_modes.shape[2] * trial_modes.shape[3] * trial_modes.shape[4]
-    count = lax.axis_size("space")
-    factor = 1.0 / (4.0 * math.sqrt(cell_count * count))
+    ns, nt, nz = lax.axis_size("space"), lax.axis_size("test"), lax.axis_size("trial")
+    factor = 1.0 / (4.0 * math.sqrt(cell_count * ns))
     order = (2, 3, 0, 1, 4)
     own = jnp.transpose(trial_modes, order)
     weighted = jnp.transpose(
         (test_modes.astype(jnp.float32) * volumes).astype(jnp.bfloat16), order
-    ).astype(jnp.float32)
-    ends = count - 1
-    padded = jnp.concatenate(
-        [
-            lax.ppermute(own[-1:], "space", [(i, i + 1) for i in range(ends)]),
-            own,
-            lax.ppermute(own[:1], "space", [(i + 1, i) for i in range(ends)]),
-        ],
-        axis=0,
     )
-    every = lax.all_gather(own, "trial", axis=3, tiled=True)
     planes, rows_each, _, modes, lanes = own.shape
     tests = weighted.shape[3]
-    total = pl.pallas_call(
-        kernel,
-        out_shape=jax.ShapeDtypeStruct((every.shape[3], tests * modes), jnp.float32),
-        in_specs=[pl.BlockSpec(memory_space=pltpu.VMEM)] * 3,
+    every = modes * nz
+    piece = every // ns
+    parts = tests // (GROUP * 4)
+    width = tests * modes // parts
+    dma = pltpu.SemaphoreType.DMA
+    mine = pl.pallas_call(
+        functools.partial(kernel, factor),
+        out_shape=jax.ShapeDtypeStruct((piece, tests * modes), jnp.float32),
+        in_specs=[pl.BlockSpec(memory_space=pltpu.VMEM)] * 2,
         out_specs=pl.BlockSpec(memory_space=pltpu.VMEM),
         scratch_shapes=[
+            pltpu.VMEM((planes + 2, rows_each, 3, modes, lanes), jnp.bfloat16),
+            pltpu.VMEM((planes, nz, rows_each, 3, modes, lanes), jnp.bfloat16),
+            pltpu.VMEM(weighted.shape, jnp.float32),
             pltpu.VMEM((planes, rows_each, 3, 3, modes, lanes), MIXED),
-            pltpu.VMEM((tests * modes, every.shape[3]), jnp.float32),
+            pltpu.VMEM((tests * modes, every), jnp.float32),
+            pltpu.VMEM((parts, ns, piece, width), jnp.float32),
+            pltpu.VMEM((parts, ns, piece, width), jnp.bfloat16),
+            pltpu.VMEM((parts, ns, piece, width), jnp.bfloat16),
+            dma((2,)),
+            dma((2,)),
+            dma((planes, nz)),
+            dma((planes, nz)),
+            dma((planes, nz)),
+            dma((planes, nz, nt)),
+            dma((planes, nz, nt)),
+            dma((parts, ns)),
+            dma((parts, ns)),
         ],
-        compiler_params=pltpu.CompilerParams(vmem_limit_bytes=48 * 2**20),
-    )(padded, every, weighted)
-    mine = lax.psum_scatter(total, "space", scatter_dimension=0, tiled=True) * factor
-    return mine.reshape(mine.shape[0], tests, modes)
+        compiler_params=pltpu.CompilerParams(
+            vmem_limit_bytes=48 * 2**20, collective_id=0, has_side_effects=True
+        ),
+    )(own, weighted)
+    return mine.reshape(piece, tests, modes)
 
 
 def solution(mesh):

time: 140 us -> 61.1 us (0.44)
  waiting for transfers between devices: 79.4 us -> 0 us
  Pallas kernels: 29.7 us -> 56.4 us
  between operations: 13.5 us -> 0.02 us
  starting transfers between devices: 6.63 us -> 0 us
  local copies, waits for them, and re-layouts: 6.88 us -> 3.11 us
  other arithmetic: 3.29 us -> 1.36 us
    all_gather x1 -> x0, waiting for transfers between devices: 52.8 us -> none  [shards(): every = lax.all_gather(own, 'trial', axis=3, tiled=True)]
    pallas_call x1, Pallas kernels: 29.7 us -> 56.4 us  [shards(): pl.pallas_call(functools.partial(kernel, factor), out_shape=jax.ShapeDtyp...]
    reduce_scatter x1 -> x0, waiting for transfers between devices: 23.7 us -> none  [shards(): lax.psum_scatter(total, 'space', scatter_dimension=0, tiled=True) * factor]
    ppermute x2 -> x0, starting transfers between devices: 6.59 us -> none  [the longest x1 4.54 us: shards(): lax.ppermute(own[-1:], 'space', [(i, i + 1) for i in range(ends)])]
    ppermute x2 -> x0, waiting for transfers between devices: 2.86 us -> none  [the longest x1 2.85 us: shards(): lax.ppermute(own[:1], 'space', [(i + 1, i) for i in range(ends)])]
    unnamed x9 -> x3, local copies, waits for them, and re-layouts: 4.37 us -> 1.64 us
    convert_element_type x1 -> x0, other arithmetic: 2.18 us -> none  [shards(): weighted = jnp.transpose((test_modes.astype(jnp.float32) * volumes).astyp...]
  transfers between devices with their start and end apart: 4 -> 0, of which waited for: 3 -> 0; matrix products, arithmetic and copies ran while one was open for 2% -> 0% of each run, Pallas kernels for 0% -> 0%
where the time goes in v2:
time: 61.1 us; the launch traced here: 60.9 us
  Pallas kernels  56.4 us (92%)
  local copies, waits for them, and re-layouts  3.11 us (5%)
  other arithmetic  1.36 us (2%)
    pallas_call x1, Pallas kernels, shards(): pl.pallas_call(functools.partial(kernel, factor), out_shape=jax.ShapeDtyp...  56.4 us
    unnamed x3, local copies, waits for them, and re-layouts  1.64 us
    reshape x2, local copies, waits for them, and re-layouts, shards(): return mine.reshape(piece, tests, modes)  1.46 us
    transpose x1, other arithmetic, shards(): jnp.transpose((test_modes.astype(jnp.float32) * volumes).astype(jnp.bfloa...  1.36 us

profile of v2, /device:TPU:1, one launch (start us, length us, event | category | flops | bytes accessed | tf_op | source)
XLA Modules:
  0.0 60.9 jit_solution(1426598044321826576)
XLA Ops:
  0.0 0.0 copy-start
  0.0 1.6 %copy.12 = bf16[3,32,4,8,128]{4,1,0,3,2:T(8,128)(2,1)S(1)} copy(bf16[3,32,4,8,128]{4,3,2,1,0:T(8,128)(2,1)} %param.4) | data formatting | bytes 1572864 | tf_op args[1]
  1.6 0.1 copy-done
  1.6 1.4 %fusion.test_ref = bf16[4,8,3,64,128]{4,3,2,1,0:T(8,128)(2,1)S(1)} fusion(bf16[3,64,4,8,128]{4,3,2,1,0:T(8,128)(2,1)S(1)} %copy-done, f32[4,8,128]{2,1,0:T(8,128)} %param.5), kind=kLoop, calls=%fused_computation.1 | loop fusion | flops 2359296 | bytes 3162112 | tf_op jit(solution)/shard_map/transpose | solution.py:333
  3.0 56.4 %shard_map.37 = f32[32,2048]{1,0:T(8,128)S(1)} custom-call(bf16[4,8,3,32,128]{4,3,2,1,0:T(8,128)(2,1)S(1)} %bitcast.5, bf16[4,8,3,64,128]{4,3,2,1,0:T(8,128)(2,1)S(1)} %fusion.test_ref), custom_call_target="tpu_custom_call" | custom-call | tf_op jit(solution)/shard_map/pallas_call | solution.py:343
  59.4 0.3 reshape.4
  59.7 1.1 %copy.9 = f32[32,64,32]{1,2,0:T(8,128)} copy(f32[32,64,32]{2,1,0:T(8,128)S(1)} %reshape.4) | data formatting | bytes 524288 | tf_op jit(solution)/shard_map/reshape | solution.py:371
Async XLA Ops:
  0.0 1.6 %copy-start = (bf16[3,64,4,8,128]{4,3,2,1,0:T(8,128)(2,1)S(1)}, bf16[3,64,4,8,128]{4,3,2,1,0:T(8,128)(2,1)}, u32[]{:S(2)}) copy-start(bf16[3,64,4,8,128]{4,3,2,1,0:T(8,128)(2,1)} %param.3) | copy-start | bytes 4718596

commit v3 on v2

--- a/solution.py
+++ b/solution.py
@@ -9,7 +9,7 @@
 from jax.sharding import PartitionSpec as P
 
 GROUP = 8
-MIXED = jnp.float32
+MIXED = jnp.bfloat16
 MESH = pl.DeviceIdType.MESH
 
 
@@ -32,6 +32,11 @@
     return along_x, along_y, along_z
 
 
+def spread(line, like):
+    tile = jnp.broadcast_to(line, (16, line.shape[1])).astype(MIXED)
+    return jnp.concatenate([tile] * (like.shape[0] // 16), axis=0)
+
+
 def pair_rows(weighted_ref, grad_ref, plane, first_row, rows, first_mode):
     columns = []
     for row in range(rows):
@@ -39,10 +44,7 @@
         per_mode = []
         for mode in range(GROUP):
             w = [
-                jnp.broadcast_to(
-                    weighted_ref[plane, first_row + row, a, pl.ds(first_mode + mode, 1), :],
-                    grads[0][0].shape,
-                ).astype(MIXED)
+                spread(weighted_ref[plane, first_row + row, a, pl.ds(first_mode + mode, 1), :], grads[0][0])
                 for a in range(3)
             ]
             per_mode.append(
@@ -217,22 +219,28 @@
         weighted_ref[plane] = test_ref[plane].astype(jnp.float32)
 
     total_ref[...] = jnp.zeros_like(total_ref)
-    for hop in range(1, nz):
-        slot(0, hop)
-
-    @pl.when(s > 0)
-    def _():
-        halo(0).wait_recv()
-
-    @pl.when(s < ns - 1)
-    def _():
-        halo(1).wait_recv()
-
-    @pl.loop(0, planes)
-    def _(plane):
+    slot(0, 1)
+
+    def find_gradients(plane):
         found = gradients_of_plane(padded_ref[plane], padded_ref[plane + 1], padded_ref[plane + 2])
         for b in range(3):
             grad_ref[plane, :, :, b] = found[b].astype(jnp.bfloat16).astype(MIXED)
+
+    pl.loop(1, planes - 1)(find_gradients)
+
+    @pl.when(s > 0)
+    def _():
+        halo(0).wait_recv()
+
+    @pl.when(s < ns - 1)
+    def _():
+        halo(1).wait_recv()
+
+    for hop in range(2, nz):
+        slot(0, hop)
+        if hop == 2:
+            for plane in sorted({0, planes - 1}):
+                find_gradients(plane)
 
     def flush(part):
         rows = span * modes
@@ -249,11 +257,14 @@
     def _(step):
         plane, m = step // (pairs * parts), step % (pairs * parts)
         last = plane == planes - 1
-        q = jnp.where(last, m % pairs, m // parts)
-        part = jnp.where(last, m // pairs, m % parts)
+        early = pairs // nt
+        late = m - early * parts
+        by_part = last & (late >= 0)
+        q = jnp.where(by_part, early + late % (pairs - early), m // parts)
+        part = jnp.where(by_part, late // (pairs - early), m % parts)
         row = lax.rem(t * share + q * 2, rows_each)
 
-        @pl.when(m == jnp.where(last, pairs // nt, pairs // nt * parts))
+        @pl.when(m == early * parts)
         def _():
             wait_across(plane)
 
@@ -279,7 +290,7 @@
             def _(hop):
                 slot(plane + 1, hop)
 
-        @pl.when(last & (m % pairs == pairs - 1))
+        @pl.when(by_part & (late % (pairs - early) == pairs - early - 1))
         def _():
             flush(part)
 

time: 61.1 us -> 54.7 us (0.90)
  Pallas kernels: 56.4 us -> 49.9 us
    pallas_call x1, Pallas kernels: 56.4 us -> 49.9 us  [shards(): pl.pallas_call(functools.partial(kernel, factor), out_shape=jax.ShapeDtyp...]
where the time goes in v3:
time: 54.7 us; the launch traced here: 54.4 us
  Pallas kernels  49.9 us (91%)
  local copies, waits for them, and re-layouts  3.11 us (6%)
  other arithmetic  1.36 us (2%)
    pallas_call x1, Pallas kernels, shards(): pl.pallas_call(functools.partial(kernel, factor), out_shape=jax.ShapeDtyp...  49.9 us
    unnamed x3, local copies, waits for them, and re-layouts  1.64 us
    reshape x2, local copies, waits for them, and re-layouts, shards(): return mine.reshape(piece, tests, modes)  1.46 us
    transpose x1, other arithmetic, shards(): jnp.transpose((test_modes.astype(jnp.float32) * volumes).astype(jnp.bfloa...  1.36 us

profile of v3, /device:TPU:1, one launch (start us, length us, event | category | flops | bytes accessed | tf_op | source)
XLA Modules:
  0.0 54.4 jit_solution(14503616506922811561)
XLA Ops:
  0.0 0.0 copy-start
  0.0 1.6 %copy.12 = bf16[3,32,4,8,128]{4,1,0,3,2:T(8,128)(2,1)S(1)} copy(bf16[3,32,4,8,128]{4,3,2,1,0:T(8,128)(2,1)} %param.4) | data formatting | bytes 1572864 | tf_op args[1]
  1.6 0.1 copy-done
  1.6 1.4 %fusion.test_ref = bf16[4,8,3,64,128]{4,3,2,1,0:T(8,128)(2,1)S(1)} fusion(bf16[3,64,4,8,128]{4,3,2,1,0:T(8,128)(2,1)S(1)} %copy-done, f32[4,8,128]{2,1,0:T(8,128)} %param.5), kind=kLoop, calls=%fused_computation.1 | loop fusion | flops 2359296 | bytes 3162112 | tf_op jit(solution)/shard_map/transpose | solution.py:344
  3.0 49.9 %shard_map.37 = f32[32,2048]{1,0:T(8,128)S(1)} custom-call(bf16[4,8,3,32,128]{4,3,2,1,0:T(8,128)(2,1)S(1)} %bitcast.5, bf16[4,8,3,64,128]{4,3,2,1,0:T(8,128)(2,1)S(1)} %fusion.test_ref), custom_call_target="tpu_custom_call" | custom-call | tf_op jit(solution)/shard_map/pallas_call | solution.py:354
  52.9 0.3 reshape.4
  53.3 1.1 %copy.9 = f32[32,64,32]{1,2,0:T(8,128)} copy(f32[32,64,32]{2,1,0:T(8,128)S(1)} %reshape.4) | data formatting | bytes 524288 | tf_op jit(solution)/shard_map/reshape | solution.py:382
Async XLA Ops:
  0.0 1.6 %copy-start = (bf16[3,64,4,8,128]{4,3,2,1,0:T(8,128)(2,1)S(1)}, bf16[3,64,4,8,128]{4,3,2,1,0:T(8,128)(2,1)}, u32[]{:S(2)}) copy-start(bf16[3,64,4,8,128]{4,3,2,1,0:T(8,128)(2,1)} %param.3) | copy-start | bytes 4718596

commit v4 on v3

--- a/solution.py
+++ b/solution.py
@@ -67,16 +67,18 @@
     tests = weighted_ref.shape[3]
     s, t, z = lax.axis_index("space"), lax.axis_index("test"), lax.axis_index("trial")
     ns, nt, nz = lax.axis_size("space"), lax.axis_size("test"), lax.axis_size("trial")
-    share = rows_each // nt
-    pairs = rows_each // 2
+    chunks, deep = all_ref.shape[0], all_ref.shape[2]
+    per_plane = chunks // planes
+    share = deep // nt
+    pairs = deep // 2
     unroll = 4
     span = GROUP * unroll
     parts = tests // span
     every = out_ref.shape[0] * ns
     piece = out_ref.shape[0]
 
-    def block(plane, source, part):
-        return all_ref.at[plane, source, pl.ds(part * share, share)]
+    def block(chunk, source, part):
+        return all_ref.at[chunk, source, pl.ds(part * share, share)]
 
     def along_line(plane, source, target, sems):
         return pltpu.make_async_remote_copy(
@@ -140,7 +142,8 @@
     def _(plane):
         here = own_ref[plane]
         padded_ref[plane + 1] = here
-        all_ref[plane, z] = here
+        for h in range(per_plane):
+            all_ref[plane * per_plane + h, z] = here[h * deep : (h + 1) * deep]
 
     sides = jnp.where(z > 0, 1, 0) + jnp.where(z < nz - 1, 1, 0)
     pl.semaphore_wait(barrier, ns - 1 + nt - 1 + sides)
@@ -180,13 +183,13 @@
                 across(plane, after, t, lax.rem(t + d, nt)).start()
 
     def slot(plane, hop):
-        @pl.when((hop == 0) & (plane + 1 < planes))
-        def _():
-            send_own(plane + 1)
-
         @pl.when(hop > 0)
         def _():
             pass_on(plane, hop)
+
+        @pl.when((hop == 1) & (plane + 2 < chunks))
+        def _():
+            send_own(plane + 2)
 
     def wait_across(plane):
         for d in range(1, nz):
@@ -195,6 +198,7 @@
                 across(plane, source, lax.rem(t + e, nt), t).wait_recv()
 
     send_own(0)
+    send_own(1)
 
     @pl.when(s < ns - 1)
     def _():
@@ -203,8 +207,6 @@
     @pl.when(s > 0)
     def _():
         halo(1).start()
-
-    slot(0, 0)
 
     @pl.when(s == 0)
     def _():
@@ -253,24 +255,26 @@
         def _(d):
             partial_to(part, lax.rem(s + d, ns)).start()
 
-    @pl.loop(0, planes * pairs * parts)
+    @pl.loop(0, chunks * pairs * parts)
     def _(step):
-        plane, m = step // (pairs * parts), step % (pairs * parts)
-        last = plane == planes - 1
+        chunk, m = step // (pairs * parts), step % (pairs * parts)
+        plane = chunk // per_plane
+        last = chunk == chunks - 1
         early = pairs // nt
         late = m - early * parts
         by_part = last & (late >= 0)
         q = jnp.where(by_part, early + late % (pairs - early), m // parts)
         part = jnp.where(by_part, late // (pairs - early), m % parts)
-        row = lax.rem(t * share + q * 2, rows_each)
+        row = lax.rem(t * share + q * 2, deep)
+        top = (chunk % per_plane) * deep + row
 
         @pl.when(m == early * parts)
         def _():
-            wait_across(plane)
+            wait_across(chunk)
 
         trial = jnp.concatenate(
             [
-                jnp.concatenate([all_ref[plane, source, row + r, b] for source in range(nz)], axis=0)
+                jnp.concatenate([all_ref[chunk, source, row + r, b] for source in range(nz)], axis=0)
                 for r in range(2)
                 for b in range(3)
             ],
@@ -278,17 +282,17 @@
         )
         for u in range(unroll):
             first = part * span + u * GROUP
-            lhs = pair_rows(weighted_ref, grad_ref, plane, row, 2, first)
+            lhs = pair_rows(weighted_ref, grad_ref, plane, top, 2, first)
             where = pl.ds(pl.multiple_of(first * modes, GROUP * modes), GROUP * modes)
             total_ref[where, :] += lax.dot_general(
                 lhs, trial, (((1,), (1,)), ((), ())), preferred_element_type=jnp.float32
             )
 
-        @pl.when((plane + 1 < planes) & (m % parts == parts - 1))
-        def _():
-            @pl.loop(m // parts * nz // pairs, (m // parts + 1) * nz // pairs)
+        @pl.when(chunk + 1 < chunks)
+        def _():
+            @pl.loop(m * nz // (pairs * parts), (m + 1) * nz // (pairs * parts))
             def _(hop):
-                slot(plane + 1, hop)
+                slot(chunk + 1, hop)
 
         @pl.when(by_part & (late % (pairs - early) == pairs - early - 1))
         def _():
@@ -304,7 +308,7 @@
 
         out_ref[:, part * width : (part + 1) * width] = turned_ref[part, s] * factor
 
-    @pl.loop(0, planes)
+    @pl.loop(0, chunks)
     def _(plane):
         @pl.loop(0, nz)
         def _(source):
@@ -350,6 +354,8 @@
     piece = every // ns
     parts = tests // (GROUP * 4)
     width = tests * modes // parts
+    halves = 2
+    chunks = planes * halves
     dma = pltpu.SemaphoreType.DMA
     mine = pl.pallas_call(
         functools.partial(kernel, factor),
@@ -358,7 +364,7 @@
         out_specs=pl.BlockSpec(memory_space=pltpu.VMEM),
         scratch_shapes=[
             pltpu.VMEM((planes + 2, rows_each, 3, modes, lanes), jnp.bfloat16),
-            pltpu.VMEM((planes, nz, rows_each, 3, modes, lanes), jnp.bfloat16),
+            pltpu.VMEM((chunks, nz, rows_each // halves, 3, modes, lanes), jnp.bfloat16),
             pltpu.VMEM(weighted.shape, jnp.float32),
             pltpu.VMEM((planes, rows_each, 3, 3, modes, lanes), MIXED),
             pltpu.VMEM((tests * modes, every), jnp.float32),
@@ -367,11 +373,11 @@
             pltpu.VMEM((parts, ns, piece, width), jnp.bfloat16),
             dma((2,)),
             dma((2,)),
-            dma((planes, nz)),
-            dma((planes, nz)),
-            dma((planes, nz)),
-            dma((planes, nz, nt)),
-            dma((planes, nz, nt)),
+            dma((chunks, nz)),
+            dma((chunks, nz)),
+            dma((chunks, nz)),
+            dma((chunks, nz, nt)),
+            dma((chunks, nz, nt)),
             dma((parts, ns)),
             dma((parts, ns)),
         ],

time: 54.7 us -> 66.5 us (1.22)
  Pallas kernels: 49.9 us -> 61.7 us
    pallas_call x1, Pallas kernels: 49.9 us -> 61.7 us  [shards(): pl.pallas_call(functools.partial(kernel, factor), out_shape=jax.ShapeDtyp...]
where the time goes in v4:
time: 66.5 us; the launch traced here: 66.2 us
  Pallas kernels  61.7 us (93%)
  local copies, waits for them, and re-layouts  3.11 us (5%)
  other arithmetic  1.36 us (2%)
    pallas_call x1, Pallas kernels, shards(): pl.pallas_call(functools.partial(kernel, factor), out_shape=jax.ShapeDtyp...  61.7 us
    unnamed x3, local copies, waits for them, and re-layouts  1.64 us
    reshape x2, local copies, waits for them, and re-layouts, shards(): return mine.reshape(piece, tests, modes)  1.46 us
    transpose x1, other arithmetic, shards(): jnp.transpose((test_modes.astype(jnp.float32) * volumes).astype(jnp.bfloa...  1.36 us

profile of v4, /device:TPU:1, one launch (start us, length us, event | category | flops | bytes accessed | tf_op | source)
XLA Modules:
  0.0 66.2 jit_solution(13283510449774049834)
XLA Ops:
  0.0 0.0 copy-start
  0.0 1.6 %copy.12 = bf16[3,32,4,8,128]{4,1,0,3,2:T(8,128)(2,1)S(1)} copy(bf16[3,32,4,8,128]{4,3,2,1,0:T(8,128)(2,1)} %param.4) | data formatting | bytes 1572864 | tf_op args[1]
  1.6 0.1 copy-done
  1.6 1.4 %fusion.test_ref = bf16[4,8,3,64,128]{4,3,2,1,0:T(8,128)(2,1)S(1)} fusion(bf16[3,64,4,8,128]{4,3,2,1,0:T(8,128)(2,1)S(1)} %copy-done, f32[4,8,128]{2,1,0:T(8,128)} %param.5), kind=kLoop, calls=%fused_computation.1 | loop fusion | flops 2359296 | bytes 3162112 | tf_op jit(solution)/shard_map/transpose | solution.py:348
  3.0 61.7 %shard_map.37 = f32[32,2048]{1,0:T(8,128)S(1)} custom-call(bf16[4,8,3,32,128]{4,3,2,1,0:T(8,128)(2,1)S(1)} %bitcast.5, bf16[4,8,3,64,128]{4,3,2,1,0:T(8,128)(2,1)S(1)} %fusion.test_ref), custom_call_target="tpu_custom_call" | custom-call | tf_op jit(solution)/shard_map/pallas_call | solution.py:360
  64.8 0.3 reshape.4
  65.1 1.1 %copy.9 = f32[32,64,32]{1,2,0:T(8,128)} copy(f32[32,64,32]{2,1,0:T(8,128)S(1)} %reshape.4) | data formatting | bytes 524288 | tf_op jit(solution)/shard_map/reshape | solution.py:388
Async XLA Ops:
  0.0 1.6 %copy-start = (bf16[3,64,4,8,128]{4,3,2,1,0:T(8,128)(2,1)S(1)}, bf16[3,64,4,8,128]{4,3,2,1,0:T(8,128)(2,1)}, u32[]{:S(2)}) copy-start(bf16[3,64,4,8,128]{4,3,2,1,0:T(8,128)(2,1)} %param.3) | copy-start | bytes 4718596

commit v5 on v4

--- a/solution.py
+++ b/solution.py
@@ -182,14 +182,16 @@
             for d in range(1, nt):
                 across(plane, after, t, lax.rem(t + d, nt)).start()
 
-    def slot(plane, hop):
-        @pl.when(hop > 0)
-        def _():
-            pass_on(plane, hop)
-
-        @pl.when((hop == 1) & (plane + 2 < chunks))
-        def _():
-            send_own(plane + 2)
+    def slot(stage, hop):
+        chunk = stage - hop + 1
+
+        @pl.when((hop > 0) & (chunk >= 0) & (chunk < chunks))
+        def _():
+            pass_on(chunk, hop)
+
+        @pl.when((hop == 1) & (stage + 2 < chunks))
+        def _():
+            send_own(stage + 2)
 
     def wait_across(plane):
         for d in range(1, nz):
@@ -238,9 +240,10 @@
     def _():
         halo(1).wait_recv()
 
-    for hop in range(2, nz):
-        slot(0, hop)
-        if hop == 2:
+    for stage in range(1, nz - 1):
+        for hop in range(min(stage + 1, nz - 1), 0, -1):
+            slot(stage, hop)
+        if stage == 1:
             for plane in sorted({0, planes - 1}):
                 find_gradients(plane)
 
@@ -288,11 +291,9 @@
                 lhs, trial, (((1,), (1,)), ((), ())), preferred_element_type=jnp.float32
             )
 
-        @pl.when(chunk + 1 < chunks)
-        def _():
-            @pl.loop(m * nz // (pairs * parts), (m + 1) * nz // (pairs * parts))
-            def _(hop):
-                slot(chunk + 1, hop)
+        @pl.loop(m * nz // (pairs * parts), (m + 1) * nz // (pairs * parts))
+        def _(turn):
+            slot(chunk + nz - 1, nz - 1 - turn)
 
         @pl.when(by_part & (late % (pairs - early) == pairs - early - 1))
         def _():

time: 66.5 us -> 55.6 us (0.84)
  Pallas kernels: 61.7 us -> 50.9 us
    pallas_call x1, Pallas kernels: 61.7 us -> 50.9 us  [shards(): pl.pallas_call(functools.partial(kernel, factor), out_shape=jax.ShapeDtyp...]
where the time goes in v5:
time: 55.6 us; the launch traced here: 55.4 us
  Pallas kernels  50.9 us (92%)
  local copies, waits for them, and re-layouts  3.11 us (6%)
  other arithmetic  1.36 us (2%)
    pallas_call x1, Pallas kernels, shards(): pl.pallas_call(functools.partial(kernel, factor), out_shape=jax.ShapeDtyp...  50.9 us
    unnamed x3, local copies, waits for them, and re-layouts  1.64 us
    reshape x2, local copies, waits for them, and re-layouts, shards(): return mine.reshape(piece, tests, modes)  1.46 us
    transpose x1, other arithmetic, shards(): jnp.transpose((test_modes.astype(jnp.float32) * volumes).astype(jnp.bfloa...  1.36 us

profile of v5, /device:TPU:1, one launch (start us, length us, event | category | flops | bytes accessed | tf_op | source)
XLA Modules:
  0.0 55.4 jit_solution(16305643137163949098)
XLA Ops:
  0.0 0.0 copy-start
  0.0 1.6 %copy.12 = bf16[3,32,4,8,128]{4,1,0,3,2:T(8,128)(2,1)S(1)} copy(bf16[3,32,4,8,128]{4,3,2,1,0:T(8,128)(2,1)} %param.4) | data formatting | bytes 1572864 | tf_op args[1]
  1.6 0.1 copy-done
  1.6 1.4 %fusion.test_ref = bf16[4,8,3,64,128]{4,3,2,1,0:T(8,128)(2,1)S(1)} fusion(bf16[3,64,4,8,128]{4,3,2,1,0:T(8,128)(2,1)S(1)} %copy-done, f32[4,8,128]{2,1,0:T(8,128)} %param.5), kind=kLoop, calls=%fused_computation.1 | loop fusion | flops 2359296 | bytes 3162112 | tf_op jit(solution)/shard_map/transpose | solution.py:349
  3.0 50.9 %shard_map.37 = f32[32,2048]{1,0:T(8,128)S(1)} custom-call(bf16[4,8,3,32,128]{4,3,2,1,0:T(8,128)(2,1)S(1)} %bitcast.5, bf16[4,8,3,64,128]{4,3,2,1,0:T(8,128)(2,1)S(1)} %fusion.test_ref), custom_call_target="tpu_custom_call" | custom-call | tf_op jit(solution)/shard_map/pallas_call | solution.py:361
  53.9 0.3 reshape.4
  54.3 1.1 %copy.9 = f32[32,64,32]{1,2,0:T(8,128)} copy(f32[32,64,32]{2,1,0:T(8,128)S(1)} %reshape.4) | data formatting | bytes 524288 | tf_op jit(solution)/shard_map/reshape | solution.py:389
Async XLA Ops:
  0.0 1.6 %copy-start = (bf16[3,64,4,8,128]{4,3,2,1,0:T(8,128)(2,1)S(1)}, bf16[3,64,4,8,128]{4,3,2,1,0:T(8,128)(2,1)}, u32[]{:S(2)}) copy-start(bf16[3,64,4,8,128]{4,3,2,1,0:T(8,128)(2,1)} %param.3) | copy-start | bytes 4718596
